TPU v7x, 512 devices: a whole 4x8x8 slice. The times are simulated.
512 devices in a mesh: occ: 32 (over z_hi, x, core), virt: 16 (over z_lo, y).
Axes of the slice: x: 4, y: 8, z: 8 (z_hi: 4, z_lo: 2; z = z_hi * 2 + z_lo), core: 2. Of those that a mesh axis runs over, the one named last changes fastest.
Arguments:
- amplitudes: bfloat16 [8192, 4096], P('occ', 'virt'), may hold values from -6 to 6
- screen: int32 [64, 32], P('occ', 'virt'), may hold values 0 or 1
- hole_ints: bfloat16 [8192, 8192], P('occ'), may hold values from -0.09375 to 0.09375
- particle_ints: bfloat16 [4096, 4096], P('virt', 'occ'), may hold values from -0.125 to 0.125
- direct_ints: bfloat16 [8192, 4096], P('occ', 'virt'), may hold values from -6 to 6
- occ_energy: float32 [8192], P('occ'), may hold values from -3 to -0.5
- virt_energy: float32 [4096], P('virt'), may hold values from 0.5 to 4
Outputs:
- residual: float32 [8192, 4096], P('occ', 'virt')
- updated: bfloat16 [8192, 4096], P('occ', 'virt')
All inputs are finite; a program needn't handle non-finite values. No bound on the sum of `screen` on one device may be relied on, other than what follows from the above.
Results may differ from a plain program's by a relative error of at most 0.001.
Values may be sent and summed in bfloat16 or wider, within the bound.
A program may use at most 64 MiB of HBM per device.

v0:
```python
import jax
import jax.numpy as jnp
from jax import lax
from jax.sharding import PartitionSpec as P


def on_device(amplitudes, screen, hole_ints, particle_ints, direct_ints, occ_energy, virt_energy):
    blocksz = amplitudes.shape[0] // screen.shape[0]
    keep = jnp.repeat(jnp.repeat(screen, blocksz, 0), blocksz, 1).astype(jnp.float32)
    amps = amplitudes.astype(jnp.float32)
    screened = (amps * keep).astype(jnp.bfloat16)
    block = lax.all_gather(screened, "occ", axis=0, tiled=True)
    hole = jnp.dot(hole_ints, block, preferred_element_type=jnp.float32)
    terms = jnp.dot(
        screened,
        lax.all_gather(particle_ints, "occ", axis=1, tiled=True),
        preferred_element_type=jnp.float32,
    )
    particle = lax.psum_scatter(terms, "virt", scatter_dimension=1, tiled=True)
    denom = virt_energy[None, :] - occ_energy[:, None]
    residual = keep * (direct_ints.astype(jnp.float32) + hole + particle - denom * amps)
    updated = (amps + residual / denom).astype(jnp.bfloat16)
    return (residual, updated)


def solution(mesh):
    in_specs = (
        P("occ", "virt"),
        P("occ", "virt"),
        P("occ", None),
        P("virt", "occ"),
        P("occ", "virt"),
        P("occ"),
        P("virt"),
    )
    out_specs = (P("occ", "virt"), P("occ", "virt"))
    return jax.shard_map(
        on_device, mesh=mesh, in_specs=in_specs, out_specs=out_specs, check_vma=False
    )
```

profile of v0, /device:TPU:4, one launch (start us, length us, event | category | flops | bytes accessed | tf_op | source)
XLA Modules:
  0.0 245.0 jit_solution(11203230014962937934)
XLA Ops:
  7.2 0.0 all-gather.5.cloned.1.call-start
  7.2 0.7 all-gather.5.cloned.1.call-update
  7.9 0.0 all-gather.3.cloned.1.call-start
  7.9 1.0 copy.11
  9.0 0.7 convert_element_type.23
  9.6 0.1 copy.9
  9.7 0.1 broadcast_bitcast_fusion
  9.8 0.7 fusion.5
  10.5 0.0 all-gather.3.cloned.1.call-update
  10.5 0.0 copy-start
  10.5 0.0 copy-start.1
  10.5 0.0 copy-start.2
  10.6 0.0 reduce-scatter.2.cloned.1.call-start
  10.6 65.7 %all-gather.5.cloned.1.call-done = bf16[256,4096]{1,0:T(8,128)(2,1)} async-done(((bf16[256,128]{1,0:T(8,128)(2,1)}), bf16[256,4096]{1,0:T(8,128)(2,1)}) %all-gather.5.cloned.1.call-update) | async-done | bytes 2097168 | tf_op jit(solution)/shard_map/all_gather | solution.py:16
  76.3 4.6 %fusion.6 = f32[256,4096]{0,1:T(8,128)} fusion(bf16[256,256]{0,1:T(8,128)(2,1)} %fusion.5, bf16[256,4096]{1,0:T(8,128)(2,1)} %all-gather.5.cloned.1.call-done), kind=kOutput, calls=%fused_computation.13 | convolution fusion | flops 536870912 | bytes 6422528 | tf_op jit(solution)/shard_map/dot_general | solution.py:14
  80.9 0.0 reduce-scatter.2.cloned.1.call-update
  80.9 0.0 copy-done
  80.9 0.1 copy.10
  81.0 67.7 %all-gather.3.cloned.1.call-done = bf16[8192,256]{0,1:T(8,128)(2,1)} async-done(((bf16[256,256]{0,1:T(8,128)(2,1)}), bf16[8192,256]{0,1:T(8,128)(2,1)}) %all-gather.3.cloned.1.call-update) | async-done | bytes 4194320 | tf_op jit(solution)/shard_map/all_gather | solution.py:12
  148.7 83.3 %reduce-scatter.2.cloned.1.call-done = f32[256,256]{0,1:T(8,128)} async-done(((f32[256,4096]{0,1:T(8,128)}), f32[256,256]{0,1:T(8,128)}) %reduce-scatter.2.cloned.1.call-update) | async-done | bytes 262160 | tf_op jit(solution)/shard_map/reduce_scatter | solution.py:19
  232.0 0.0 copy-done.1
  232.1 4.8 %fusion.4 = (bf16[256,256]{0,1:T(8,128)(2,1)S(1)}, f32[256,256]{0,1:T(8,128)S(1)}) fusion(bf16[256,256]{0,1:T(8,128)(2,1)S(1)} %copy.11, f32[256]{0:T(256)S(1)} %copy-done.1, f32[256]{0:T(256)S(1)} %copy-done.2, f32[256,256]{0,1:T(8,128)S(1)} %bitcast.25, f32[256,256]{0,1:T(8,128)} %reduce-scatter.2.cloned.1.call-done, ...), kind=kOutput, calls=%fused_computation.9 | convolution fusion | flops 1074462720 | bytes 9570304 | tf_op jit(solution)/shard_map/dot_general | solution.py:13
  236.8 0.8 copy.13
  237.7 0.8 copy.14
  (3 shorter events, 0.0 us)
Async XLA Ops:
  7.2 69.1 %all-gather.5.cloned.1.call-start = ((), (), s32[]{:S(2)}) async-start(), calls=%async_computation.2 | async-start | bytes 2162688 | tf_op jit(solution)/shard_map/all_gather | solution.py:16
  7.9 140.8 %all-gather.3.cloned.1.call-start = ((), (), s32[]{:S(2)}) async-start(), calls=%async_computation.1 | async-start | bytes 4325376 | tf_op jit(solution)/shard_map/all_gather | solution.py:12
  10.5 70.4 %copy-start = (bf16[256,256]{1,0:T(8,128)(2,1)S(1)}, bf16[256,256]{1,0:T(8,128)(2,1)}, u32[]{:S(2)}) copy-start(bf16[256,256]{1,0:T(8,128)(2,1)} %param.11) | copy-start | bytes 393220
  10.5 221.5 %copy-start.1 = (f32[256]{0:T(256)S(1)}, f32[256]{0:T(256)}, u32[]{:S(2)}) copy-start(f32[256]{0:T(256)} %param.12) | copy-start | bytes 3076
  10.5 221.5 %copy-start.2 = (f32[256]{0:T(256)S(1)}, f32[256]{0:T(256)}, u32[]{:S(2)}) copy-start(f32[256]{0:T(256)} %param.13) | copy-start | bytes 3076
  10.6 221.5 %reduce-scatter.2.cloned.1.call-start = ((), (), s32[]{:S(2)}) async-start(), calls=%async_computation.3 | async-start | bytes 4456448 | tf_op jit(solution)/shard_map/reduce_scatter | solution.py:19
Sparse Core Ops, SparseCore 0:
  11.0 65.1 all-gather.4
  79.9 68.7 all-gather.2
  151.6 80.4 reduce-scatter.1
where the time goes:
time: 245 us
  waiting for transfers between devices  217 us (89%)
  between operations  13.8 us (6%)
  matrix products  9.38 us (4%)
  local copies, waits for them, and re-layouts  2.91 us (1%)
    reduce_scatter x1, waiting for transfers between devices, on_device(): particle = lax.psum_scatter(terms, 'virt', scatter_dimension=1, tiled=True)  83.3 us
    all_gather x1, waiting for transfers between devices, on_device(): block = lax.all_gather(screened, 'occ', axis=0, tiled=True)  67.7 us
    all_gather x1, waiting for transfers between devices, on_device(): lax.all_gather(particle_ints, 'occ', axis=1, tiled=True)  65.7 us
  transfers between devices with their start and end apart: 3, of which 3 were waited for; matrix products, arithmetic and copies ran while one was open for 3% of the time, Pallas kernels for 0%

commit v1 on v0

v1 whole, which is shorter than its diff:
```python
import functools

import jax
import jax.numpy as jnp
from jax import lax
from jax.experimental import pallas as pl
from jax.experimental.pallas import tpu as pltpu
from jax.sharding import PartitionSpec as P

MESH = pl.DeviceIdType.MESH
NX, NZH, NY, NZL = 4, 4, 8, 2
ROWS, COLS, HALF, TILE = 256, 256, 128, 128


def wrap(a, n):
    return lax.rem(a + n, n)


class Links:
    def __init__(self, send_sem, recv_sem):
        self.send_sem, self.recv_sem = send_sem, recv_sem
        self.ids, self.sent = {}, []

    def _copy(self, name, src, dst, device):
        n = self.ids.setdefault(name, len(self.ids))
        return pltpu.make_async_remote_copy(
            src_ref=src,
            dst_ref=dst,
            send_sem=self.send_sem.at[n],
            recv_sem=self.recv_sem.at[n],
            device_id=device,
            device_id_type=MESH,
        )

    def send(self, name, src, device, dst=None):
        copy = self._copy(name, src, src if dst is None else dst, device)
        copy.start()
        self.sent.append(copy)

    def recv(self, name, dst, device):
        self._copy(name, dst, dst, device).wait_recv()

    def drain(self):
        for copy in self.sent:
            copy.wait_send()


N_COPIES = 96


def kernel(
    screen_ref,
    amps_hbm,
    hole_hbm,
    part_hbm,
    direct_hbm,
    occ_ref,
    virt_ref,
    residual_ref,
    updated_ref,
    amps,
    direct,
    hole_ints,
    col,
    row,
    slab,
    total,
    send_sem,
    recv_sem,
    load_sem,
):
    o, v = lax.axis_index("occ"), lax.axis_index("virt")
    core, chip = lax.rem(o, 2), o // 2
    x, zh = lax.rem(chip, NX), chip // NX
    zl, y = v // NY, lax.rem(v, NY)

    def occ_of(zh, x, core):
        return (zh * NX + x) * 2 + core

    def zx(dz, dx):
        return wrap(zh + dz, NZH), wrap(x + dx, NX)

    def at_zx(dz, dx):
        return (occ_of(*zx(dz, dx), core), v)

    def at_y(dy):
        return (o, zl * NY + wrap(y + dy, NY))

    sibling = (occ_of(zh, x, 1 - core), v)
    partner = (o, (1 - zl) * NY + y)
    across = (v * 2 + core, chip)
    moves = chip != v

    load_amps = pltpu.make_async_copy(amps_hbm, amps, load_sem.at[0])
    load_amps.start()
    load_hole = pltpu.make_async_copy(hole_hbm, hole_ints, load_sem.at[1])
    load_direct = pltpu.make_async_copy(direct_hbm, direct, load_sem.at[2])
    load_hole.start()
    load_direct.start()

    barrier = pltpu.get_barrier_semaphore()
    near = [at_zx(1, 0), at_zx(-1, 0), at_zx(0, 1), at_zx(0, -1), at_y(1), at_y(-1), sibling, partner]
    for device in near:
        pl.semaphore_signal(barrier, inc=1, device_id=device, device_id_type=MESH)

    @pl.when(moves)
    def _():
        pl.semaphore_signal(barrier, inc=1, device_id=across, device_id_type=MESH)

    load_amps.wait()
    for i in range(2):
        for j in range(2):
            rows, cols = pl.ds(i * TILE, TILE), pl.ds(j * TILE, TILE)
            keep = screen_ref[i, j].astype(jnp.float32)
            tile = (amps[rows, cols].astype(jnp.float32) * keep).astype(jnp.bfloat16)
            col[o, rows, cols] = tile
            row[v, rows, cols] = tile

    pl.semaphore_wait(barrier, len(near) + moves.astype(jnp.int32))

    links = Links(send_sem, recv_sem)
    home = slab.at[core, chip]

    @pl.when(moves)
    def _():
        links._copy("across", part_hbm, slab.at[core, v], across).start()

    @pl.when(jnp.logical_not(moves))
    def _():
        pltpu.make_async_copy(part_hbm, home, load_sem.at[3]).start()

    class Gather:
        def __init__(self, tag, block):
            self.tag, self.block = tag, block

        def full(self, dz, dx):
            return self.block(*zx(dz, dx), core)

        def half(self, dz, dx, h):
            return self.full(dz, dx).at[pl.ds(h * HALF, HALF)]

        def name(self, *parts):
            return (self.tag,) + parts

        def z0(self):
            links.send(self.name("zf"), self.full(0, 0), at_zx(1, 0))
            links.send(self.name("zb"), self.full(0, 0), at_zx(-1, 0))

        def z1(self, way):
            tag = "f" if way == 1 else "b"
            h = 0 if way == 1 else 1
            links.recv(self.name("z" + tag), self.full(-way, 0), at_zx(-way, 0))
            links.send(self.name("zh" + tag), self.half(-way, 0, h), at_zx(way, 0))

        def z2(self):
            links.recv(self.name("zhf"), self.half(2, 0, 0), at_zx(-1, 0))
            links.recv(self.name("zhb"), self.half(2, 0, 1), at_zx(1, 0))

        def x0(self, dz):
            links.send(self.name("xf", dz), self.full(dz, 0), at_zx(0, 1))
            links.send(self.name("xb", dz), self.full(dz, 0), at_zx(0, -1))
            self.sib(dz, 0)

        def x1(self, dz):
            for way, tag, h in ((1, "f", 0), (-1, "b", 1)):
                links.recv(self.name("x" + tag, dz), self.full(dz, -way), at_zx(0, -way))
                links.send(self.name("xh" + tag, dz), self.half(dz, -way, h), at_zx(0, way))
            self.sib(dz, -1)
            self.sib(dz, 1)

        def x2(self, dz):
            links.recv(self.name("xhf", dz), self.half(dz, 2, 0), at_zx(0, -1))
            links.recv(self.name("xhb", dz), self.half(dz, 2, 1), at_zx(0, 1))
            self.sib(dz, 2)

        def sib(self, dz, dx):
            links.send(self.name("s", dz, dx), self.full(dz, dx), sibling)

        def from_sib(self, dz, dx):
            links.recv(self.name("s", dz, dx), self.block(*zx(dz, dx), 1 - core), sibling)

    amp = Gather("T", lambda zh, x, c: col.at[occ_of(zh, x, c)])
    ints = Gather("P", lambda zh, x, c: slab.at[c, zh * NX + x])

    def strip(e, dy):
        return row.at[(zl if e == 0 else 1 - zl) * NY + wrap(y + dy, NY)]

    def strip_half(e, dy, h):
        return strip(e, dy).at[pl.ds(h * HALF, HALF)]

    def y_send(e, hop):
        links.send(("y", e, hop, "f"), strip(e, 1 - hop), at_y(1))
        links.send(("y", e, hop, "b"), strip(e, hop - 1), at_y(-1))

    def y_recv(e, hop):
        links.recv(("y", e, hop, "f"), strip(e, -hop), at_y(-1))
        links.recv(("y", e, hop, "b"), strip(e, hop), at_y(1))

    def y_send_last(e):
        links.send(("y", e, 4, "f"), strip_half(e, -3, 0), at_y(1))
        links.send(("y", e, 4, "b"), strip_half(e, 3, 1), at_y(-1))

    def y_recv_last(e):
        links.recv(("y", e, 4, "f"), strip_half(e, 4, 0), at_y(-1))
        links.recv(("y", e, 4, "b"), strip_half(e, 4, 1), at_y(1))

    def add_hole(dz, dx):
        amp.from_sib(dz, dx)
        zz, xx = zx(dz, dx)
        c = zz * NX + xx
        block = col[pl.ds(c * 2, 2)].reshape(2 * ROWS, COLS)
        ints_ = hole_ints[:, pl.ds(pl.multiple_of(c * 512, 512), 512)]
        total[...] += jnp.dot(ints_, block, preferred_element_type=jnp.float32)

    amp.x0(0)
    amp.z0()
    y_send(0, 1)
    links.send(("pair",), row.at[v], partner)
    total[...] = jnp.zeros_like(total)
    amp.x1(0)
    y_recv(0, 1)
    y_send(0, 2)
    links.recv(("pair",), row.at[(1 - zl) * NY + y], partner)
    y_send(1, 1)
    amp.z1(1)
    amp.x0(-1)
    amp.z1(-1)
    amp.x0(1)

    @pl.when(moves)
    def _():
        links.recv("across", home, across)

    @pl.when(jnp.logical_not(moves))
    def _():
        pltpu.make_async_copy(part_hbm, home, load_sem.at[3]).wait()

    ints.z0()
    ints.x0(0)
    y_recv(1, 1)
    y_send(1, 2)
    y_recv(0, 2)
    y_send(0, 3)
    amp.x1(-1)
    amp.z2()
    amp.x0(2)
    load_hole.wait()
    add_hole(0, 0)
    y_recv(1, 2)
    y_send(1, 3)
    amp.x1(1)
    ints.x1(0)
    ints.z1(1)
    ints.x0(-1)
    ints.z1(-1)
    ints.x0(1)
    amp.x2(0)
    y_recv(0, 3)
    y_send_last(0)
    add_hole(0, 1)
    add_hole(0, -1)
    add_hole(-1, 0)
    add_hole(1, 0)
    amp.x1(2)
    ints.z2()
    ints.x0(2)
    y_recv(1, 3)
    y_send_last(1)
    amp.x2(-1)
    amp.x2(1)
    add_hole(-1, -1)
    add_hole(-1, 1)
    add_hole(0, 2)
    add_hole(2, 0)
    ints.x1(-1)
    ints.x1(1)
    add_hole(1, -1)
    add_hole(1, 1)
    add_hole(2, -1)
    add_hole(2, 1)
    ints.x2(0)
    amp.x2(2)
    ints.x1(2)
    ints.x2(-1)
    ints.x2(1)
    ints.x2(2)
    y_recv_last(0)
    y_recv_last(1)
    add_hole(-1, 2)
    add_hole(1, 2)
    add_hole(2, 2)
    for dz in (0, -1, 1, 2):
        for dx in (0, -1, 1, 2):
            ints.from_sib(dz, dx)

    for c in range(2):
        cols = pl.ds(c * TILE, TILE)

        def body(k, acc, c=c):
            return acc + jnp.dot(row[k], slab[c, k], preferred_element_type=jnp.float32)

        total[:, cols] = lax.fori_loop(0, 16, body, total[:, cols])

    load_direct.wait()
    occ_col = jnp.transpose(jnp.broadcast_to(occ_ref[...], (TILE, ROWS)))
    for i in range(2):
        for j in range(2):
            rows, cols = pl.ds(i * TILE, TILE), pl.ds(j * TILE, TILE)
            keep = screen_ref[i, j].astype(jnp.float32)
            a = amps[rows, cols].astype(jnp.float32)
            denom = virt_ref[:, cols] - occ_col[i * TILE : (i + 1) * TILE]
            res = keep * (direct[rows, cols].astype(jnp.float32) + total[rows, cols] - denom * a)
            residual_ref[rows, cols] = res
            updated_ref[rows, cols] = (a + res / denom).astype(jnp.bfloat16)

    @pl.when(moves)
    def _():
        links._copy("across", part_hbm, home, across).wait_send()

    links.drain()
    assert len(links.ids) <= N_COPIES


def on_device(amplitudes, screen, hole_ints, particle_ints, direct_ints, occ_energy, virt_energy):
    vmem, hbm = pl.BlockSpec(memory_space=pltpu.VMEM), pl.BlockSpec(memory_space=pl.ANY)
    return pl.pallas_call(
        kernel,
        out_shape=(
            jax.ShapeDtypeStruct((ROWS, COLS), jnp.float32),
            jax.ShapeDtypeStruct((ROWS, COLS), jnp.bfloat16),
        ),
        in_specs=[pl.BlockSpec(memory_space=pltpu.SMEM), hbm, hbm, hbm, hbm, vmem, vmem],
        out_specs=(vmem, vmem),
        scratch_shapes=[
            pltpu.VMEM((ROWS, COLS), jnp.bfloat16),
            pltpu.VMEM((ROWS, COLS), jnp.bfloat16),
            pltpu.VMEM((ROWS, 8192), jnp.bfloat16),
            pltpu.VMEM((32, ROWS, COLS), jnp.bfloat16),
            pltpu.VMEM((16, ROWS, COLS), jnp.bfloat16),
            pltpu.VMEM((2, 16, ROWS, TILE), jnp.bfloat16),
            pltpu.VMEM((ROWS, COLS), jnp.float32),
            pltpu.SemaphoreType.DMA((N_COPIES,)),
            pltpu.SemaphoreType.DMA((N_COPIES,)),
            pltpu.SemaphoreType.DMA((4,)),
        ],
        compiler_params=pltpu.CompilerParams(
            collective_id=0, has_side_effects=True, vmem_limit_bytes=40 * 2**20
        ),
        name="ladders",
    )(
        screen,
        amplitudes,
        hole_ints,
        particle_ints,
        direct_ints,
        occ_energy.reshape(1, ROWS),
        virt_energy.reshape(1, COLS),
    )


def solution(mesh):
    in_specs = (
        P("occ", "virt"),
        P("occ", "virt"),
        P("occ", None),
        P("virt", "occ"),
        P("occ", "virt"),
        P("occ"),
        P("virt"),
    )
    out_specs = (P("occ", "virt"), P("occ", "virt"))
    return jax.shard_map(
        on_device, mesh=mesh, in_specs=in_specs, out_specs=out_specs, check_vma=False
    )
```

time: 245 us -> 73 us (0.30)
  the two profiles are of different devices: /device:TPU:4 before, /device:TPU:27 now
where the time goes in v1:
time: 73 us; the launch traced here: 72.7 us
  Pallas kernels  63.8 us (87%)
  local copies, waits for them, and re-layouts  8.22 us (11%)
    pallas_call x1, Pallas kernels, on_device(): pl.pallas_call(kernel, out_shape=(jax.ShapeDtypeStruct((ROWS, COLS), jnp....  63.8 us
    unnamed x16, local copies, waits for them, and re-layouts  8.22 us

profile of v1, /device:TPU:27, one launch (start us, length us, event | category | flops | bytes accessed | tf_op | source)
XLA Modules:
  0.0 72.7 jit_solution(15131435489672655590)
XLA Ops:
  0.6 0.0 copy-start
  0.6 2.2 %copy-done = bf16[256,8192]{1,0:T(8,128)(2,1)S(1)} copy-done((bf16[256,8192]{1,0:T(8,128)(2,1)S(1)}, bf16[256,8192]{1,0:T(8,128)(2,1)}, u32[]{:S(2)}) %copy-start) | copy-done | bytes 4194328
  2.8 0.0 copy-start.1
  2.8 0.9 %copy-done.1 = bf16[256,256]{1,0:T(8,128)(2,1)S(1)} copy-done((bf16[256,256]{1,0:T(8,128)(2,1)S(1)}, bf16[256,256]{1,0:T(8,128)(2,1)}, u32[]{:S(2)}) %copy-start.1) | copy-done | bytes 131096
  3.7 0.0 copy-start.2
  3.7 0.9 %copy-done.2 = bf16[256,256]{1,0:T(8,128)(2,1)S(1)} copy-done((bf16[256,256]{1,0:T(8,128)(2,1)S(1)}, bf16[256,256]{1,0:T(8,128)(2,1)}, u32[]{:S(2)}) %copy-start.2) | copy-done | bytes 131096
  4.6 0.0 copy-start.3
  4.6 0.8 %copy-done.3 = bf16[256,128]{1,0:T(8,128)(2,1)S(1)} copy-done((bf16[256,128]{1,0:T(8,128)(2,1)S(1)}, bf16[256,128]{1,0:T(8,128)(2,1)}, u32[]{:S(2)}) %copy-start.3) | copy-done | bytes 65560
  5.5 0.0 copy-start.4
  5.5 0.7 copy-done.4
  6.2 0.0 copy-start.5
  6.2 0.7 copy-done.5
  6.8 0.0 copy-start.6
  6.8 0.7 copy-done.6
  7.5 63.8 %ladders.1 = (f32[256,256]{1,0:T(8,128)S(1)}, bf16[256,256]{1,0:T(8,128)(2,1)S(1)}) custom-call(s32[2,2]{1,0:T(2,128)S(1)} %copy-done.4, bf16[256,256]{1,0:T(8,128)(2,1)S(1)} %copy-done.1, bf16[256,8192]{1,0:T(8,128)(2,1)S(1)} %copy-done, bf16[256,128]{1,0:T(8,128)(2,1)S(1)} %copy-done.3, bf16[256,256]{1,0:T(8,128)(2,1)S(1)} %copy-done.2, ...), custom_call_target="tpu_custom_call" | custom-call | tf_op jit(solution)/shard_map/ladders/pallas_call | solution.py:326
  71.3 0.7 copy.11
  72.1 0.7 copy.12
Async XLA Ops:
  0.6 2.2 %copy-start = (bf16[256,8192]{1,0:T(8,128)(2,1)S(1)}, bf16[256,8192]{1,0:T(8,128)(2,1)}, u32[]{:S(2)}) copy-start(bf16[256,8192]{1,0:T(8,128)(2,1)} %hole_hbm.1) | copy-start | bytes 12582916
  2.8 0.9 %copy-start.1 = (bf16[256,256]{1,0:T(8,128)(2,1)S(1)}, bf16[256,256]{1,0:T(8,128)(2,1)}, u32[]{:S(2)}) copy-start(bf16[256,256]{1,0:T(8,128)(2,1)} %amps_hbm.1) | copy-start | bytes 393220
  3.7 0.9 %copy-start.2 = (bf16[256,256]{1,0:T(8,128)(2,1)S(1)}, bf16[256,256]{1,0:T(8,128)(2,1)}, u32[]{:S(2)}) copy-start(bf16[256,256]{1,0:T(8,128)(2,1)} %direct_hbm.1) | copy-start | bytes 393220
  4.6 0.8 %copy-start.3 = (bf16[256,128]{1,0:T(8,128)(2,1)S(1)}, bf16[256,128]{1,0:T(8,128)(2,1)}, u32[]{:S(2)}) copy-start(bf16[256,128]{1,0:T(8,128)(2,1)} %part_hbm.1) | copy-start | bytes 196612
  5.5 0.7 copy-start.4
  6.2 0.7 copy-start.5
  6.8 0.7 copy-start.6

commit v2 on v0

v2 whole, which is shorter than its diff:
```python
import functools

import jax
import jax.numpy as jnp
from jax import lax
from jax.experimental import pallas as pl
from jax.experimental.pallas import tpu as pltpu
from jax.sharding import PartitionSpec as P

MESH = pl.DeviceIdType.MESH
NX, NZH, NY, NZL = 4, 4, 8, 2
ROWS, COLS, HALF, TILE = 256, 256, 128, 128


def wrap(a, n):
    return lax.rem(a + n, n)


class Links:
    KINDS = "Typ12"

    def __init__(self, send_sem, recv_sem):
        self.send_sem, self.recv_sem = send_sem, recv_sem
        self.ids, self.sent = {}, {}

    def copy(self, name, src, dst, device):
        n = self.ids.setdefault(name, len(self.ids))
        return pltpu.make_async_remote_copy(
            src_ref=src,
            dst_ref=dst,
            send_sem=self.send_sem.at[self.KINDS.index(name[0][0])],
            recv_sem=self.recv_sem.at[n],
            device_id=device,
            device_id_type=MESH,
        )

    def send(self, name, src, device):
        self.copy(name, src, src, device).start()
        self.sent[name] = src.shape[0] * src.shape[1]

    def recv(self, name, dst, device):
        self.copy(name, dst, dst, device).wait_recv()

    def drain(self, kind, everything, device):
        sent = sum(size for name, size in self.sent.items() if name[0][0] == kind)
        assert sent == everything.shape[0] * everything.shape[1] * everything.shape[2]
        self.copy((kind,), everything, everything, device).wait_send()


N_COPIES = 112


def kernel(
    screen_hbm,
    amps_hbm,
    hole_hbm,
    part_hbm,
    direct_hbm,
    occ_hbm,
    virt_hbm,
    residual_ref,
    updated_ref,
    amps,
    direct,
    hole_ints,
    col,
    row,
    slab,
    moved,
    total,
    occ_ref,
    virt_ref,
    screen,
    send_sem,
    recv_sem,
    load_sem,
    z_sem,
):
    o, v = lax.axis_index("occ"), lax.axis_index("virt")
    core, chip = lax.rem(o, 2), o // 2
    x, zh = lax.rem(chip, NX), chip // NX
    zl, y = v // NY, lax.rem(v, NY)
    yl, y2 = lax.rem(y, 4), y // 4

    def occ_of(zh, x, core):
        return (zh * NX + x) * 2 + core

    def zx(dz, dx):
        return wrap(zh + dz, NZH), wrap(x + dx, NX)

    def at_zx(dz, dx):
        return (occ_of(*zx(dz, dx), core), v)

    def at_y(dy):
        return (o, zl * NY + wrap(y + dy, NY))

    def flipped(zh, hi, lo):
        return lax.rem(zh // 2 + hi, 2) * 2 + lax.rem(zh + lo, 2)

    sibling = (occ_of(zh, x, 1 - core), v)
    partner = (o, (1 - zl) * NY + y)
    zh_1 = flipped(zh, zl, y2)
    first_to = (occ_of(zh_1, wrap(x + yl, NX), core), v)
    first_from = (occ_of(zh_1, wrap(x - yl, NX), core), v)
    first_moves = v != 0
    v_2 = lax.rem(zh // 2 + zl, 2) * NY + lax.rem(zh + y2, 2) * 4 + wrap(x - yl, 4)
    second = (o, v_2)
    second_moves = v_2 != v

    def signal(sem, device):
        pl.semaphore_signal(sem, inc=1, device_id=device, device_id_type=MESH)

    first_plane = v + zh * 16 < NY
    later_plane = jnp.logical_not(first_plane)
    from_first = (zl == 0) & (zh == 1) & (y2 == 1)
    to_later = first_plane & (y2 == 1)
    barrier = pltpu.get_barrier_semaphore()
    plane = [at_zx(0, 1), at_zx(0, -1), at_y(1), at_y(-1), sibling]
    across = [
        (at_zx(1, 0), (zl == 0) & (zh == NZH - 1)),
        (at_zx(-1, 0), (zl == 0) & (zh == 1)),
        (partner, (zl == 1) & (zh == 0)),
    ]
    pl.when(first_moves & jnp.logical_not(from_first))(lambda: signal(barrier, first_from))
    pl.when(to_later)(lambda: signal(barrier, first_to))
    pl.when(second_moves)(lambda: signal(barrier, second))
    for device, to_first in across:
        pl.when(jnp.logical_not(to_first))(lambda device=device: signal(barrier, device))
    for device in plane:
        signal(barrier, device)

    loads = [
        pltpu.make_async_copy(src, dst, load_sem.at[n])
        for n, (src, dst) in enumerate(
            (
                (amps_hbm, amps),
                (hole_hbm, hole_ints),
                (direct_hbm, direct),
                (occ_hbm, occ_ref),
                (virt_hbm, virt_ref),
                (screen_hbm, screen),
            )
        )
    ]
    for load in loads:
        load.start()
    loads[0].wait()
    loads[5].wait()
    for i in range(2):
        for j in range(2):
            rows, cols = pl.ds(i * TILE, TILE), pl.ds(j * TILE, TILE)
            keep = screen[i : i + 1, j : j + 1].astype(jnp.float32)
            tile = (amps[rows, cols].astype(jnp.float32) * keep).astype(jnp.bfloat16)
            col[o, rows, cols] = tile
            row[v, rows, cols] = tile

    def count(*flags):
        return sum(flag.astype(jnp.int32) for flag in flags)

    pl.semaphore_wait(
        barrier,
        len(plane)
        + len(across) * count(later_plane)
        + count(first_moves & jnp.logical_not(to_later), second_moves, from_first),
    )
    for device, to_first in across:
        pl.when(to_first)(lambda device=device: signal(z_sem, device))
    pl.when(from_first)(lambda: signal(z_sem, first_from))

    links = Links(send_sem, recv_sem)

    WAYS = ((1, "f", 0), (-1, "b", 1))

    def amp(dz, dx, h=None, c=None):
        ref = col.at[occ_of(*zx(dz, dx), core if c is None else c)]
        return ref if h is None else ref.at[pl.ds(h * HALF, HALF)]

    def z_own():
        for late in range(2):
            for way, tag, h in WAYS:
                h = h if late == 0 else 1 - h
                links.send(("Tz", tag, h), amp(0, 0, h), at_zx(way, 0))

    def x_send(dz, h):
        for way, tag, _ in WAYS:
            links.send(("Tx", dz, tag, h), amp(dz, 0, h), at_zx(0, way))

    def x_own():
        for late in range(2):
            for way, tag, h in WAYS:
                h = h if late == 0 else 1 - h
                links.send(("Tx", 0, tag, h), amp(0, 0, h), at_zx(0, way))
        to_sib(0, 0)

    def z_on(late):
        for way, tag, h in WAYS:
            h = h if late == 0 else 1 - h
            links.recv(("Tz", tag, h), amp(-way, 0, h), at_zx(-way, 0))
            if late == 0:
                links.send(("Tzz", tag), amp(-way, 0, h), at_zx(way, 0))
            x_send(-way, h)
            if late == 1:
                to_sib(-way, 0)

    def z_far():
        for way, tag, h in WAYS:
            links.recv(("Tzz", tag), amp(2, 0, h), at_zx(-way, 0))
            x_send(2, h)
        to_sib(2, 0)

    def x_on(dz):
        for way, tag, h in WAYS:
            links.recv(("Tx", dz, tag, h), amp(dz, -way, h), at_zx(0, -way))
            links.send(("Txx", dz, tag), amp(dz, -way, h), at_zx(0, way))

    def x_rest(dz):
        for way, tag, h in WAYS:
            links.recv(("Tx", dz, tag, 1 - h), amp(dz, -way, 1 - h), at_zx(0, -way))
            to_sib(dz, -way)

    def x_far(dz):
        for way, tag, h in WAYS:
            links.recv(("Txx", dz, tag), amp(dz, 2, h), at_zx(0, -way))
        to_sib(dz, 2)

    def to_sib(dz, dx):
        links.send(("Ts", dz, dx), amp(dz, dx), sibling)

    def add_hole(dz, dx):
        links.recv(("Ts", dz, dx), amp(dz, dx, c=1 - core), sibling)
        zz, xx = zx(dz, dx)
        c = zz * NX + xx
        block = col[pl.ds(c * 2, 2)].reshape(2 * ROWS, COLS)
        ints_ = hole_ints[:, pl.ds(pl.multiple_of(c * 512, 512), 512)]
        total[...] += jnp.dot(ints_, block, preferred_element_type=jnp.float32)

    def ints(dz, dx, h=None, c=None):
        zz, xx = zx(dz, dx)
        ref = slab.at[(core if c is None else c) * 16 + zz * NX + xx]
        return ref if h is None else ref.at[pl.ds(h * HALF, HALF)]

    def p_z():
        for way, tag, h in WAYS:
            links.send(("pz", tag), ints(0, 0), at_zx(way, 0))

    def p_x(dz):
        for way, tag, h in WAYS:
            links.send(("px", dz, tag), ints(dz, 0), at_zx(0, way))
        links.send(("ps", dz, 0), ints(dz, 0), sibling)

    def p_z_on():
        for way, tag, h in WAYS:
            links.recv(("pz", tag), ints(-way, 0), at_zx(-way, 0))
            links.send(("pzz", tag), ints(-way, 0, h), at_zx(way, 0))
            p_x(-way)

    def p_z_far():
        for way, tag, h in WAYS:
            links.recv(("pzz", tag), ints(2, 0, h), at_zx(-way, 0))
        p_x(2)

    def p_x_on(dz):
        for way, tag, h in WAYS:
            links.recv(("px", dz, tag), ints(dz, -way), at_zx(0, -way))
            links.send(("pxx", dz, tag), ints(dz, -way, h), at_zx(0, way))
            links.send(("ps", dz, -way), ints(dz, -way), sibling)

    def p_x_far(dz):
        for way, tag, h in WAYS:
            links.recv(("pxx", dz, tag), ints(dz, 2, h), at_zx(0, -way))
        links.send(("ps", dz, 2), ints(dz, 2), sibling)

    def add_particle(dz, dx):
        links.recv(("ps", dz, dx), ints(dz, dx, c=1 - core), sibling)
        zz, xx = zx(dz, dx)
        p = zz * NX + xx
        k = lax.rem(zz // 2 + zl, 2) * NY + lax.rem(zz + y2, 2) * 4 + wrap(xx - yl, 4)
        block = jnp.concatenate([slab[p], slab[16 + p]], axis=1)
        total[...] += jnp.dot(row[k], block, preferred_element_type=jnp.float32)

    def strip(e, dy, h=None):
        ref = row.at[(zl if e == 0 else 1 - zl) * NY + wrap(y + dy, NY)]
        return ref if h is None else ref.at[pl.ds(h * HALF, HALF)]

    def y_send(e, hop):
        for way, tag, h in WAYS:
            if hop < 4:
                links.send(("y", e, hop, tag), strip(e, -way * (hop - 1)), at_y(way))
            else:
                links.send(("y", e, hop, tag), strip(e, -way * 3, h), at_y(way))

    def y_recv(e, hop):
        for way, tag, h in WAYS:
            if hop < 4:
                links.recv(("y", e, hop, tag), strip(e, -way * hop), at_y(-way))
            else:
                links.recv(("y", e, hop, tag), strip(e, 4, h), at_y(-way))

    def y_on(e, hop):
        y_recv(e, hop)
        y_send(e, hop + 1)

    def move(name, src, dst, to, come_from, moves, sem):
        def start():
            @pl.when(moves)
            def _():
                links.copy((name,), src, dst, to).start()

            @pl.when(jnp.logical_not(moves))
            def _():
                pltpu.make_async_copy(src, dst, sem).start()

        def arrive():
            @pl.when(moves)
            def _():
                links.copy((name,), src, dst, come_from).wait_recv()

            @pl.when(jnp.logical_not(moves))
            def _():
                pltpu.make_async_copy(src, dst, sem).wait()

        def leave():
            @pl.when(moves)
            def _():
                links.copy((name,), src, dst, to).wait_send()

        return start, arrive, leave

    first = move("1", part_hbm, moved, first_to, first_from, first_moves, load_sem.at[6])
    second_ = move("2", moved, ints(0, 0), second, second, second_moves, load_sem.at[7])

    def step(name, fn, *args, when=None):
        if when is None:
            fn(*args)
        else:
            pl.when(when)(lambda: fn(*args))

    step("first0", first[0], when=jnp.logical_not(to_later))
    step("x_own", x_own)
    step("e_y01", y_send, 0, 1, when=first_plane)
    step("e_x_on", x_on, 0, when=first_plane)
    step("e_y1", y_on, 0, 1, when=first_plane)
    step("e_x_rest", x_rest, 0, when=first_plane)
    step("e_x_far", x_far, 0, when=first_plane)
    step("z_sem", lambda: pl.semaphore_wait(z_sem, len(across) + count(to_later)), when=first_plane)
    step("first0", first[0], when=to_later)
    step("z_own", z_own)
    step("y01", y_send, 0, 1, when=later_plane)
    total[...] = jnp.zeros_like(total)
    step("x_on0", x_on, 0, when=later_plane)
    step("first_in", first[1])
    step("second", second_[0])
    step("y_on01", y_on, 0, 1, when=later_plane)
    step("x_rest0", x_rest, 0, when=later_plane)
    step("z_on0", z_on, 0)
    step("x_far0", x_far, 0, when=later_plane)
    step("pair", lambda: links.send(("ypair",), row.at[v], partner))
    step("z_on1", z_on, 1)
    step("y_on02", y_on, 0, 2)
    step("second_in", second_[1])
    step("p_z", p_z)
    step("p_x0", p_x, 0)
    step("x_on-1", x_on, -1)
    step("x_on1", x_on, 1)
    step("z_far", z_far)
    step("pair_recv", lambda: links.recv(("ypair",), strip(1, 0), partner))
    step("y11", y_send, 1, 1)
    step("load", loads[1].wait)
    step("h00", add_hole, 0, 0)
    step("h01", add_hole, 0, 1)
    step("h0-1", add_hole, 0, -1)
    step("x_rest-1", x_rest, -1)
    step("x_rest1", x_rest, 1)
    step("y_on03", y_on, 0, 3)
    step("p_z_on", p_z_on)
    step("p_x_on0", p_x_on, 0)
    step("x_far-1", x_far, -1)
    step("x_far1", x_far, 1)
    step("x_on2", x_on, 2)
    step("y_on11", y_on, 1, 1)
    step("p_z_far", p_z_far)
    step("h02", add_hole, 0, 2)
    step("h-10", add_hole, -1, 0)
    step("h10", add_hole, 1, 0)
    step("x_rest2", x_rest, 2)
    step("x_far2", x_far, 2)
    step("y_on12", y_on, 1, 2)
    step("p_x_on-1", p_x_on, -1)
    step("p_x_on1", p_x_on, 1)
    for dz, dx in ((-1, -1), (-1, 1), (1, -1), (1, 1), (2, 0)):
        step(f"h{dz}{dx}", add_hole, dz, dx)
    step("y_on13", y_on, 1, 3)
    step("p_x_far0", p_x_far, 0)
    step("p_x_on2", p_x_on, 2)
    for dz, dx in ((-1, 2), (1, 2), (2, -1), (2, 1), (2, 2)):
        step(f"h{dz}{dx}", add_hole, dz, dx)
    step("p_x_far-1", p_x_far, -1)
    step("p_x_far1", p_x_far, 1)
    step("y04", y_recv, 0, 4)
    step("y14", y_recv, 1, 4)
    step("p_x_far2", p_x_far, 2)
    for dz in (0, -1, 1, 2):
        for dx in (0, -1, 1, 2):
            step(f"p{dz}{dx}", add_particle, dz, dx)

    def finish():
        for load in loads[2:5]:
            load.wait()
        occ_col = jnp.transpose(jnp.broadcast_to(occ_ref[...], (TILE, ROWS)))
        for i in range(2):
            for j in range(2):
                rows, cols = pl.ds(i * TILE, TILE), pl.ds(j * TILE, TILE)
                keep = screen[i : i + 1, j : j + 1].astype(jnp.float32)
                a = amps[rows, cols].astype(jnp.float32)
                denom = virt_ref[:, cols] - occ_col[i * TILE : (i + 1) * TILE]
                ladders = total[rows, cols]
                res = keep * (direct[rows, cols].astype(jnp.float32) + ladders - denom * a)
                residual_ref[rows, cols] = res
                updated_ref[rows, cols] = (a + res / denom).astype(jnp.bfloat16)

    step("finish", finish)
    step("leave1", first[2])
    step("leave2", second_[2])
    step("drainT", links.drain, "T", col.at[pl.ds(0, 31)], sibling)
    step("drainy", links.drain, "y", row.at[pl.ds(0, 15)], sibling)
    step("drainp", links.drain, "p", slab.at[pl.ds(0, 31)], sibling)
    assert len(links.ids) <= N_COPIES


def on_device(amplitudes, screen, hole_ints, particle_ints, direct_ints, occ_energy, virt_energy):
    vmem, hbm = pl.BlockSpec(memory_space=pltpu.VMEM), pl.BlockSpec(memory_space=pltpu.HBM)
    return pl.pallas_call(
        kernel,
        out_shape=(
            jax.ShapeDtypeStruct((ROWS, COLS), jnp.float32),
            jax.ShapeDtypeStruct((ROWS, COLS), jnp.bfloat16),
        ),
        in_specs=[hbm] * 7,
        out_specs=(vmem, vmem),
        scratch_shapes=[
            pltpu.VMEM((ROWS, COLS), jnp.bfloat16),
            pltpu.VMEM((ROWS, COLS), jnp.bfloat16),
            pltpu.VMEM((ROWS, 8192), jnp.bfloat16),
            pltpu.VMEM((32, ROWS, COLS), jnp.bfloat16),
            pltpu.VMEM((16, ROWS, COLS), jnp.bfloat16),
            pltpu.VMEM((32, ROWS, TILE), jnp.bfloat16),
            pltpu.VMEM((ROWS, TILE), jnp.bfloat16),
            pltpu.VMEM((ROWS, COLS), jnp.float32),
            pltpu.VMEM((1, ROWS), jnp.float32),
            pltpu.VMEM((1, COLS), jnp.float32),
            pltpu.VMEM((2, 2), jnp.int32),
            pltpu.SemaphoreType.DMA((5,)),
            pltpu.SemaphoreType.DMA((N_COPIES,)),
            pltpu.SemaphoreType.DMA((8,)),
            pltpu.SemaphoreType.REGULAR,
        ],
        compiler_params=pltpu.CompilerParams(
            collective_id=0, has_side_effects=True, vmem_limit_bytes=62 * 2**20
        ),
        name="ladders",
    )(
        screen,
        amplitudes,
        hole_ints,
        particle_ints,
        direct_ints,
        occ_energy.reshape(1, ROWS),
        virt_energy.reshape(1, COLS),
    )


def solution(mesh):
    in_specs = (
        P("occ", "virt"),
        P("occ", "virt"),
        P("occ", None),
        P("virt", "occ"),
        P("occ", "virt"),
        P("occ"),
        P("virt"),
    )
    out_specs = (P("occ", "virt"), P("occ", "virt"))
    return jax.shard_map(
        on_device, mesh=mesh, in_specs=in_specs, out_specs=out_specs, check_vma=False
    )
```

time: 245 us -> 59.8 us (0.24)
  the two profiles are of different devices: /device:TPU:4 before, /device:TPU:1 now
where the time goes in v2:
time: 59.8 us; the launch traced here: 59.7 us
  Pallas kernels  55.8 us (93%)
  local copies, waits for them, and re-layouts  3.24 us (5%)
  between operations  0.64 us (1%)
    pallas_call x1, Pallas kernels, on_device(): pl.pallas_call(kernel, out_shape=(jax.ShapeDtypeStruct((ROWS, COLS), jnp....  55.8 us
    unnamed x2, local copies, waits for them, and re-layouts  3.24 us

profile of v2, /device:TPU:1, one launch (start us, length us, event | category | flops | bytes accessed | tf_op | source)
XLA Modules:
  0.0 59.7 jit_solution(8200460284469939772)
XLA Ops:
  0.6 55.8 %ladders.1 = (f32[256,256]{1,0:T(8,128)}, bf16[256,256]{1,0:T(8,128)(2,1)}) custom-call(s32[2,2]{1,0:T(2,128)} %screen_hbm.1, bf16[256,256]{1,0:T(8,128)(2,1)} %amps_hbm.1, bf16[256,8192]{1,0:T(8,128)(2,1)} %hole_hbm.1, bf16[256,128]{1,0:T(8,128)(2,1)} %part_hbm.1, bf16[256,256]{1,0:T(8,128)(2,1)} %direct_hbm.1, f32[1,256]{1,0:T(1,128)} %bitcast.2, ...), custom_call_target="tpu_custom_call" | custom-call | tf_op jit(solution)/shard_map/ladders/pallas_call | solution.py:432
  56.4 1.7 %copy.11 = f32[256,256]{1,0:T(8,128)} copy(f32[256,256]{1,0:T(8,128)} %get-tuple-element.4) | data formatting | bytes 524288
  58.1 1.6 %copy.12 = bf16[256,256]{1,0:T(8,128)(2,1)} copy(bf16[256,256]{1,0:T(8,128)(2,1)} %get-tuple-element.5) | data formatting | bytes 262144

commit v3 on v0

v3 whole, which is shorter than its diff:
```python
import math

import jax
import jax.numpy as jnp
from jax import lax
from jax.experimental import pallas as pl
from jax.experimental.pallas import tpu as pltpu
from jax.sharding import PartitionSpec as P

MESH = pl.DeviceIdType.MESH
NX, NZH, NY, NZL = 4, 4, 8, 2
ROWS, COLS, HALF, TILE = 256, 256, 128, 128


def wrap(a, n):
    return lax.rem(a + n, n)


class Links:
    KINDS = "TOqySRp12"
    ON_CORE_0 = "TOqy"

    def __init__(self, send_sem, recv_sem):
        self.send_sem, self.recv_sem = send_sem, recv_sem
        self.ids, self.sent = ({}, {}), {}

    def copy(self, name, src, dst, device):
        ids = self.ids[name[0][0] not in self.ON_CORE_0]
        n = ids.setdefault(name, len(ids))
        return pltpu.make_async_remote_copy(
            src_ref=src,
            dst_ref=dst,
            send_sem=self.send_sem.at[self.KINDS.index(name[0][0])],
            recv_sem=self.recv_sem.at[n],
            device_id=device,
            device_id_type=MESH,
        )

    def send(self, name, src, device, dst=None):
        self.copy(name, src, src if dst is None else dst, device).start()
        self.sent[name] = math.prod(src.shape)

    def recv(self, name, dst, device):
        self.copy(name, dst, dst, device).wait_recv()

    def drain(self, kind, everything, device):
        sent = sum(size for name, size in self.sent.items() if name[0][0] == kind)
        assert sent == math.prod(everything.shape)
        name = next(name for name in self.sent if name[0][0] == kind)
        self.copy(name, everything, everything, device).wait_send()


N_COPIES = 80


def kernel(
    screen_hbm,
    amps_hbm,
    hole_hbm,
    part_hbm,
    direct_hbm,
    occ_hbm,
    virt_hbm,
    residual_ref,
    updated_ref,
    amps,
    direct,
    hole_ints,
    col,
    row,
    slab,
    moved,
    total,
    occ_ref,
    virt_ref,
    screen,
    send_sem,
    recv_sem,
    load_sem,
):
    o, v = lax.axis_index("occ"), lax.axis_index("virt")
    core, chip = lax.rem(o, 2), o // 2
    x, zh = lax.rem(chip, NX), chip // NX
    zl, y = v // NY, lax.rem(v, NY)
    yl, y2 = lax.rem(y, 4), y // 4

    def occ_of(zh, x, core):
        return (zh * NX + x) * 2 + core

    def zx(dz, dx):
        return wrap(zh + dz, NZH), wrap(x + dx, NX)

    def at_zx(dz, dx):
        return (occ_of(*zx(dz, dx), core), v)

    def at_y(dy):
        return (o, zl * NY + wrap(y + dy, NY))

    def flipped(zh, hi, lo):
        return lax.rem(zh // 2 + hi, 2) * 2 + lax.rem(zh + lo, 2)

    sibling = (occ_of(zh, x, 1 - core), v)
    partner = (o, (1 - zl) * NY + y)
    zh_1 = flipped(zh, zl, y2)
    first_to = (occ_of(zh_1, wrap(x + yl, NX), 1), v)
    first_from = [(occ_of(zh_1, wrap(x - yl, NX), c), v) for c in range(2)]
    first_moves = v != 0
    v_2 = lax.rem(zh // 2 + zl, 2) * NY + lax.rem(zh + y2, 2) * 4 + wrap(x - yl, 4)
    second = (o, v_2)
    second_moves = v_2 != v
    lead, other = core == 0, core == 1

    def signal(sem, device):
        pl.semaphore_signal(sem, inc=1, device_id=device, device_id_type=MESH)

    def count(*flags):
        return sum(flag.astype(jnp.int32) for flag in flags)

    loads = [
        pltpu.make_async_copy(src, dst, load_sem.at[n])
        for n, (src, dst) in enumerate(
            (
                (amps_hbm, amps),
                (hole_hbm, hole_ints),
                (direct_hbm, direct),
                (occ_hbm, occ_ref),
                (virt_hbm, virt_ref),
                (screen_hbm, screen),
            )
        )
    ]
    loads[0].start()
    loads[5].start()

    barrier = pltpu.get_barrier_semaphore()
    for device in first_from:
        pl.when(other & first_moves)(lambda device=device: signal(barrier, device))
    pl.when(other & second_moves)(lambda: signal(barrier, second))
    for device in (at_zx(1, 0), at_zx(-1, 0), at_zx(0, 1), at_zx(0, -1), sibling):
        signal(barrier, device)
    for device in (at_y(1), at_y(-1), partner):
        pl.when(lead)(lambda device=device: signal(barrier, device))

    for load in loads[1:5]:
        load.start()
    loads[0].wait()
    loads[5].wait()
    for i in range(2):
        for j in range(2):
            rows, cols = pl.ds(i * TILE, TILE), pl.ds(j * TILE, TILE)
            keep = screen[i : i + 1, j : j + 1].astype(jnp.float32)
            tile = (amps[rows, cols].astype(jnp.float32) * keep).astype(jnp.bfloat16)
            col[o, rows, cols] = tile
            row[v * 2 + core, rows, cols] = tile

    pl.semaphore_wait(barrier, 5 + 3 * count(lead) + count(first_moves, other & second_moves))

    links = Links(send_sem, recv_sem)

    WAYS = ((1, "f", 0), (-1, "b", 1))

    def amp(dz, dx, h=None):
        zz, xx = zx(dz, dx)
        c = (zz * NX + xx) * 2
        return col.at[pl.ds(c, 2)] if h is None else col.at[c + h]


    def to_sib(dz, dx):
        links.send(("S", dz, dx), amp(dz, dx), sibling)

    def z_send(way, tag, h):
        links.send(("Tz", tag, h), amp(0, 0, h), at_zx(way, 0))

    def x_send(dz, h):
        for way, tag, _ in WAYS:
            links.send(("Tx", dz, tag, h), amp(dz, 0, h), at_zx(0, way))

    def x0_send(way, tag, h):
        links.send(("Tx", 0, tag, h), amp(0, 0, h), at_zx(0, way))

    def x_recv(dz, way, tag, h):
        links.recv(("Tx", dz, tag, h), amp(dz, -way, h), at_zx(0, -way))

    def x_pass(dz, way, tag, h):
        links.send(("Txx", dz, tag), amp(dz, -way, h), at_zx(0, way))

    def z_first():
        for way, tag, h in WAYS:
            links.recv(("Tz", tag, h), amp(-way, 0, h), at_zx(-way, 0))
            links.send(("Tzz", tag), amp(-way, 0, h), at_zx(way, 0))
            x_send(-way, h)

    def z_rest():
        for way, tag, h in WAYS:
            links.recv(("Tz", tag, 1 - h), amp(-way, 0, 1 - h), at_zx(-way, 0))
            x_send(-way, 1 - h)
        for way, _, _ in WAYS:
            to_sib(-way, 0)

    def z_far():
        for way, tag, h in WAYS:
            links.recv(("Tzz", tag), amp(2, 0, h), at_zx(-way, 0))
        for way, tag, h in WAYS:
            links.send(("Tx", 2, tag), amp(2, 0), at_zx(0, way))
        to_sib(2, 0)

    def x0_first():
        for way, tag, h in WAYS:
            x_recv(0, way, tag, h)
            x_pass(0, way, tag, h)

    def x0_rest():
        for way, tag, h in WAYS:
            x_recv(0, way, tag, 1 - h)
            to_sib(0, -way)

    def x1_first():
        for dz, early in ((-1, 0), (1, 1)):
            for way, tag, h in WAYS:
                x_recv(dz, way, tag, early)
                if h == early:
                    x_pass(dz, way, tag, h)

    def x1_rest():
        for dz, early in ((-1, 0), (1, 1)):
            for way, tag, h in WAYS:
                x_recv(dz, way, tag, 1 - early)
                if h != early:
                    x_pass(dz, way, tag, h)
            for way, _, _ in WAYS:
                to_sib(dz, -way)

    def x2_all():
        for way, tag, h in WAYS:
            links.recv(("Tx", 2, tag), amp(2, -way), at_zx(0, -way))
            x_pass(2, way, tag, h)
            to_sib(2, -way)

    def x_far(dz):
        for way, tag, h in WAYS:
            links.recv(("Txx", dz, tag), amp(dz, 2, h), at_zx(0, -way))
        to_sib(dz, 2)


    def turned(a, b, h):
        return (a, b) if h == 0 else (b, a)

    def ints(dz, dx, h=None, part=None):
        zz, xx = zx(dz, dx)
        p = (zz * NX + xx) * 2
        ref = slab.at[pl.ds(p, 2)] if h is None else slab.at[p + h]
        return ref if part is None else ref.at[pl.ds(part * HALF, HALF)]

    def p_send(a):
        for half in range(2):
            for way, tag, _ in WAYS:
                links.send(("pb", a, half, tag), ints(*turned(a, 0, half), half), at_zx(*turned(0, way, half)))

    def p_own():
        for half in range(2):
            for way, tag, _ in WAYS:
                links.send(("pa", half, tag), ints(0, 0, half), at_zx(*turned(way, 0, half)))
        p_send(0)

    def pa_all():
        for half in range(2):
            for way, tag, h in WAYS:
                here = turned(-way, 0, half)
                links.recv(("pa", half, tag), ints(*here, half), at_zx(*here))
                links.send(("paa", half, tag), ints(*here, half, h), at_zx(*turned(way, 0, half)))
        for way, _, _ in WAYS:
            p_send(-way)

    def pa_far():
        for half in range(2):
            for way, tag, h in WAYS:
                links.recv(
                    ("paa", half, tag), ints(*turned(2, 0, half), half, h), at_zx(*turned(-way, 0, half))
                )
        p_send(2)

    def pb_all(a):
        for half in range(2):
            for way, tag, h in WAYS:
                here = turned(a, -way, half)
                links.recv(("pb", a, half, tag), ints(*here, half), at_zx(*turned(0, -way, half)))
                links.send(("pbb", a, half, tag), ints(*here, half, h), at_zx(*turned(0, way, half)))

    def pb_far(a):
        for half in range(2):
            for way, tag, h in WAYS:
                links.recv(
                    ("pbb", a, half, tag),
                    ints(*turned(a, 2, half), half, h),
                    at_zx(*turned(0, -way, half)),
                )

    def p_sibs(*places):
        for place in places:
            links.send(("q",) + place, ints(*place), sibling)

    def strip(e, dy, h=None):
        k = ((zl if e == 0 else 1 - zl) * NY + wrap(y + dy, NY)) * 2
        return row.at[pl.ds(k, 2)] if h is None else row.at[k + h]

    def y_send(e, hop, half):
        for way, tag, h in WAYS:
            if hop < 4 or h == half:
                dst = strip(e, -way * (hop - 1), half)
                src = amp(0, 0, half) if (e, hop) == (0, 1) else dst
                links.send(("y", e, hop, tag, half), src, at_y(way), dst)

    def y_on(e, hop, half):
        for way, tag, h in WAYS:
            if hop < 4 or h == half:
                links.recv(("y", e, hop, tag, half), strip(e, -way * hop, half), at_y(-way))
        if hop < 4:
            y_send(e, hop + 1, half)
        if half == 1:
            for dy in (hop, -hop) if hop < 4 else (4,):
                row_sib(e, dy)

    def row_sib(e, dy):
        links.send(("R", e, dy), strip(e, dy, 1), sibling)

    def pair_send(half):
        links.send(("ypair", half), amp(0, 0, half), partner, strip(0, 0, half))

    def pair_on(half):
        links.recv(("ypair", half), strip(1, 0, half), partner)
        y_send(1, 1, half)
        if half == 1:
            row_sib(1, 0)


    def add_hole(dz, dx, block):
        zz, xx = zx(dz, dx)
        ints_ = hole_ints[:, pl.ds(pl.multiple_of((zz * NX + xx) * 512, 512), 512)]
        total[...] += jnp.dot(
            ints_, block[...].reshape(2 * ROWS, COLS), preferred_element_type=jnp.float32
        )

    def take_holes(*places):
        for place in places:
            add_hole(*place, amp(*place))

    def get_holes(*places):
        for place in places:
            if place != (0, 0):
                links.recv(("S",) + place, amp(*place), sibling)
            add_hole(*place, amp(*place))

    def add_particle(dz, dx):
        zz, xx = zx(dz, dx)
        p = (zz * NX + xx) * 2
        k = lax.rem(zz // 2 + zl, 2) * NY + lax.rem(zz + y2, 2) * 4 + wrap(xx - yl, 4)
        block = jnp.concatenate([slab[p], slab[p + 1]], axis=1)
        total[...] += jnp.dot(row[k * 2 + core], block, preferred_element_type=jnp.float32)

    def take_particles(*places):
        for place in places:
            add_particle(*place)

    def get_rows():
        for e in range(2):
            for dy in range(e == 0, NY):
                links.recv(("R", e, dy if dy <= 4 else dy - NY), strip(e, dy, 1), sibling)

    def get_particles(*places):
        for place in places:
            links.recv(("q",) + place, ints(*place), sibling)
            add_particle(*place)


    def first():
        pl.when(lead)(lambda: links.send(("1", 0), part_hbm, first_to, moved.at[0]))
        pl.when(other & first_moves)(lambda: links.send(("1", 1), part_hbm, first_to, moved.at[1]))
        pl.when(other & jnp.logical_not(first_moves))(
            lambda: pltpu.make_async_copy(part_hbm, moved.at[1], load_sem.at[6]).start()
        )

    def first_in():
        links.recv(("1", 0), moved.at[0], first_from[0])
        pl.when(first_moves)(lambda: links.recv(("1", 1), moved.at[1], first_from[1]))
        pl.when(jnp.logical_not(first_moves))(
            lambda: pltpu.make_async_copy(part_hbm, moved.at[1], load_sem.at[6]).wait()
        )

    def second_out():
        pl.when(second_moves)(lambda: links.send(("2",), moved, second, ints(0, 0)))
        pl.when(jnp.logical_not(second_moves))(
            lambda: pltpu.make_async_copy(moved, ints(0, 0), load_sem.at[7]).start()
        )

    def second_in():
        pl.when(second_moves)(lambda: links.recv(("2",), ints(0, 0), second))
        pl.when(jnp.logical_not(second_moves))(
            lambda: pltpu.make_async_copy(moved, ints(0, 0), load_sem.at[7]).wait()
        )

    def step(name, fn, *args, when=None):
        if when is None:
            fn(*args)
        else:
            pl.when(when)(lambda: fn(*args))

    total[...] = jnp.zeros_like(total)

    def program_0():
        step("first", first)
        step("x0_send", x0_send, 1, "f", 0)
        step("z_send", z_send, 1, "f", 0)
        step("y_own0", y_send, 0, 1, 0)
        step("pair0", pair_send, 0)
        step("own_sib", lambda: links.send(("S",), amp(0, 0, 0), sibling))
        step("own_sib_in", lambda: links.recv(("O",), amp(0, 0, 1), sibling))
        step("x0_send", x0_send, -1, "b", 1)
        step("z_send", z_send, -1, "b", 1)
        step("x0_send", x0_send, 1, "f", 1)
        step("z_send", z_send, 1, "f", 1)
        step("x0_send", x0_send, -1, "b", 0)
        step("z_send", z_send, -1, "b", 0)
        step("pair1", pair_send, 1)
        step("y_own1", y_send, 0, 1, 1)
        step("y01a", y_on, 0, 1, 0)
        step("x0", x0_first)
        step("y01b", y_on, 0, 1, 1)
        step("x0r", x0_rest)
        step("pair0", pair_on, 0)
        step("z_first", z_first)
        step("y02a", y_on, 0, 2, 0)
        step("pair1", pair_on, 1)
        step("y02b", y_on, 0, 2, 1)
        step("xf0", x_far, 0)
        step("z_rest", z_rest)
        step("y11a", y_on, 1, 1, 0)
        step("x1", x1_first)
        step("y03a", y_on, 0, 3, 0)
        step("load", loads[1].wait)
        step("h0", take_holes, (0, 0), (0, -1), (0, 1), (0, 2))
        step("y11b", y_on, 1, 1, 1)
        step("y03b", y_on, 0, 3, 1)
        step("z_far", z_far)
        step("y12a", y_on, 1, 2, 0)
        step("x1r", x1_rest)
        step("h1", take_holes, (-1, 0), (1, 0), (2, 0))
        step("y12b", y_on, 1, 2, 1)
        step("y04", y_on, 0, 4, 0)
        step("y04", y_on, 0, 4, 1)
        step("h2", take_holes, (-1, -1), (-1, 1), (1, -1), (1, 1))
        step("y13a", y_on, 1, 3, 0)
        step("x2", x2_all)
        step("y13b", y_on, 1, 3, 1)
        step("h2", take_holes, (2, -1), (2, 1))
        step("xf-1", x_far, -1)
        step("xf1", x_far, 1)
        step("h3", take_holes, (-1, 2), (1, 2))
        step("y14", y_on, 1, 4, 0)
        step("y14", y_on, 1, 4, 1)
        step("p0", get_particles, (0, 0), (-1, 0), (1, 0), (0, -1), (0, 1), (0, 2), (2, 0))
        step("xf2", x_far, 2)
        step("p1", get_particles, (-1, -1), (-1, 1), (1, -1), (1, 1))
        step("h3", take_holes, (2, 2))
        step("p2", get_particles, (-1, 2), (1, 2), (2, -1), (2, 1))
        step("p3", get_particles, (2, 2))

    def program_1():
        step("first", first)
        step("own_sib", lambda: links.send(("O",), amp(0, 0, 1), sibling))
        step("own_sib_in", lambda: links.recv(("S",), amp(0, 0, 0), sibling))
        step("first_in", first_in)
        step("second", second_out)
        step("load", loads[1].wait)
        step("h0", get_holes, (0, 0), (0, -1), (0, 1), (0, 2))
        step("second_in", second_in)
        step("p_own", p_own)
        step("ps0", p_sibs, (0, 0))
        step("h1", get_holes, (-1, 0), (1, 0))
        step("pa", pa_all)
        step("pb0", pb_all, 0)
        step("ps1", p_sibs, (0, 1), (0, -1), (1, 0), (-1, 0))
        step("h1", get_holes, (2, 0))
        step("pa_far", pa_far)
        step("pbb0", pb_far, 0)
        step("ps2", p_sibs, (0, 2), (2, 0))
        step("pb-1", pb_all, -1)
        step("pb1", pb_all, 1)
        step("ps3", p_sibs, (-1, -1), (-1, 1), (1, -1), (1, 1))
        step("h2", get_holes, (-1, -1), (-1, 1), (1, -1), (1, 1))
        step("pb2", pb_all, 2)
        step("pbb-1", pb_far, -1)
        step("pbb1", pb_far, 1)
        step("ps4", p_sibs, (-1, 2), (1, 2), (2, -1), (2, 1))
        step("h3", get_holes, (2, -1), (2, 1))
        step("pbb2", pb_far, 2)
        step("ps5", p_sibs, (2, 2))
        step("h3", get_holes, (-1, 2), (1, 2))
        step("rows", get_rows)
        step("p0", take_particles, (0, 0), (-1, 0), (1, 0), (0, -1), (0, 1), (0, 2), (2, 0))
        step("p1", take_particles, (-1, -1), (-1, 1), (1, -1), (1, 1))
        step("p2", take_particles, (-1, 2), (1, 2), (2, -1), (2, 1), (2, 2))
        step("h3", get_holes, (2, 2))

    def drain_0():
        links.drain("T", col.at[pl.ds(0, 30)], sibling)
        links.drain("S", col.at[pl.ds(0, 31)], sibling)
        links.drain("y", row.at[pl.ds(0, 30)], sibling)
        links.drain("R", row.at[pl.ds(0, 15)], sibling)

    def drain_1():
        links.drain("O", col.at[pl.ds(0, 1)], sibling)
        links.drain("p", slab.at[pl.ds(0, 30)], sibling)
        links.drain("q", slab, sibling)
        pl.when(second_moves)(lambda: links.copy(("2",), moved, moved, sibling).wait_send())

    pl.when(lead)(program_0)
    pl.when(other)(program_1)

    def finish():
        for load in loads[2:5]:
            load.wait()
        occ_col = jnp.transpose(jnp.broadcast_to(occ_ref[...], (TILE, ROWS)))
        for i in range(2):
            for j in range(2):
                rows, cols = pl.ds(i * TILE, TILE), pl.ds(j * TILE, TILE)
                keep = screen[i : i + 1, j : j + 1].astype(jnp.float32)
                a = amps[rows, cols].astype(jnp.float32)
                denom = virt_ref[:, cols] - occ_col[i * TILE : (i + 1) * TILE]
                ladders = total[rows, cols]
                res = keep * (direct[rows, cols].astype(jnp.float32) + ladders - denom * a)
                residual_ref[rows, cols] = res
                updated_ref[rows, cols] = (a + res / denom).astype(jnp.bfloat16)

    step("finish", finish)
    pl.when(lead)(drain_0)
    pl.when(other)(drain_1)
    pl.when(lead | first_moves)(lambda: links.copy(("1", 0), moved.at[0], moved.at[0], sibling).wait_send())
    assert max(map(len, links.ids)) <= N_COPIES


def on_device(amplitudes, screen, hole_ints, particle_ints, direct_ints, occ_energy, virt_energy):
    vmem, hbm = pl.BlockSpec(memory_space=pltpu.VMEM), pl.BlockSpec(memory_space=pltpu.HBM)
    return pl.pallas_call(
        kernel,
        out_shape=(
            jax.ShapeDtypeStruct((ROWS, COLS), jnp.float32),
            jax.ShapeDtypeStruct((ROWS, COLS), jnp.bfloat16),
        ),
        in_specs=[hbm] * 7,
        out_specs=(vmem, vmem),
        scratch_shapes=[
            pltpu.VMEM((ROWS, COLS), jnp.bfloat16),
            pltpu.VMEM((ROWS, COLS), jnp.bfloat16),
            pltpu.VMEM((ROWS, 8192), jnp.bfloat16),
            pltpu.VMEM((32, ROWS, COLS), jnp.bfloat16),
            pltpu.VMEM((32, ROWS, COLS), jnp.bfloat16),
            pltpu.VMEM((32, ROWS, TILE), jnp.bfloat16),
            pltpu.VMEM((2, ROWS, TILE), jnp.bfloat16),
            pltpu.VMEM((ROWS, COLS), jnp.float32),
            pltpu.VMEM((1, ROWS), jnp.float32),
            pltpu.VMEM((1, COLS), jnp.float32),
            pltpu.VMEM((2, 2), jnp.int32),
            pltpu.SemaphoreType.DMA((9,)),
            pltpu.SemaphoreType.DMA((N_COPIES,)),
            pltpu.SemaphoreType.DMA((8,)),
        ],
        compiler_params=pltpu.CompilerParams(
            collective_id=0, has_side_effects=True, vmem_limit_bytes=62 * 2**20
        ),
        name="ladders",
    )(
        screen,
        amplitudes,
        hole_ints,
        particle_ints,
        direct_ints,
        occ_energy.reshape(1, ROWS),
        virt_energy.reshape(1, COLS),
    )


def solution(mesh):
    in_specs = (
        P("occ", "virt"),
        P("occ", "virt"),
        P("occ", None),
        P("virt", "occ"),
        P("occ", "virt"),
        P("occ"),
        P("virt"),
    )
    out_specs = (P("occ", "virt"), P("occ", "virt"))
    return jax.shard_map(
        on_device, mesh=mesh, in_specs=in_specs, out_specs=out_specs, check_vma=False
    )
```

time: 245 us -> 54.7 us (0.22)
  the two profiles are of different devices: /device:TPU:4 before, /device:TPU:1 now
where the time goes in v3:
time: 54.7 us; the launch traced here: 54.5 us
  Pallas kernels  50.7 us (93%)
  local copies, waits for them, and re-layouts  3.24 us (6%)
  between operations  0.64 us (1%)
    pallas_call x1, Pallas kernels, on_device(): pl.pallas_call(kernel, out_shape=(jax.ShapeDtypeStruct((ROWS, COLS), jnp....  50.7 us
    unnamed x2, local copies, waits for them, and re-layouts  3.24 us

profile of v3, /device:TPU:1, one launch (start us, length us, event | category | flops | bytes accessed | tf_op | source)
XLA Modules:
  0.0 54.5 jit_solution(4085712601850152613)
XLA Ops:
  0.6 50.7 %ladders.1 = (f32[256,256]{1,0:T(8,128)}, bf16[256,256]{1,0:T(8,128)(2,1)}) custom-call(s32[2,2]{1,0:T(2,128)} %screen_hbm.1, bf16[256,256]{1,0:T(8,128)(2,1)} %amps_hbm.1, bf16[256,8192]{1,0:T(8,128)(2,1)} %hole_hbm.1, bf16[256,128]{1,0:T(8,128)(2,1)} %part_hbm.1, bf16[256,256]{1,0:T(8,128)(2,1)} %direct_hbm.1, f32[1,256]{1,0:T(1,128)} %bitcast.2, ...), custom_call_target="tpu_custom_call" | custom-call | tf_op jit(solution)/shard_map/ladders/pallas_call | solution.py:543
  51.3 1.7 %copy.11 = f32[256,256]{1,0:T(8,128)} copy(f32[256,256]{1,0:T(8,128)} %get-tuple-element.4) | data formatting | bytes 524288
  53.0 1.6 %copy.12 = bf16[256,256]{1,0:T(8,128)(2,1)} copy(bf16[256,256]{1,0:T(8,128)(2,1)} %get-tuple-element.5) | data formatting | bytes 262144

commit v4 on v3

--- a/solution.py
+++ b/solution.py
@@ -61,8 +61,7 @@
     direct_hbm,
     occ_hbm,
     virt_hbm,
-    residual_ref,
-    updated_ref,
+    step_ref,
     amps,
     direct,
     hole_ints,
@@ -350,16 +349,23 @@
                 links.recv(("S",) + place, amp(*place), sibling)
             add_hole(*place, amp(*place))
 
-    def add_particle(dz, dx):
-        zz, xx = zx(dz, dx)
-        p = (zz * NX + xx) * 2
-        k = lax.rem(zz // 2 + zl, 2) * NY + lax.rem(zz + y2, 2) * 4 + wrap(xx - yl, 4)
-        block = jnp.concatenate([slab[p], slab[p + 1]], axis=1)
-        total[...] += jnp.dot(row[k * 2 + core], block, preferred_element_type=jnp.float32)
+    def add_particles(places):
+        rows, blocks = [], []
+        for dz, dx in places:
+            zz, xx = zx(dz, dx)
+            p = (zz * NX + xx) * 2
+            k = lax.rem(zz // 2 + zl, 2) * NY + lax.rem(zz + y2, 2) * 4 + wrap(xx - yl, 4)
+            rows.append(row[k * 2 + core])
+            blocks.append(jnp.concatenate([slab[p], slab[p + 1]], axis=1))
+        total[...] += jnp.dot(
+            jnp.concatenate(rows, axis=1),
+            jnp.concatenate(blocks, axis=0),
+            preferred_element_type=jnp.float32,
+        )
 
     def take_particles(*places):
-        for place in places:
-            add_particle(*place)
+        for n in range(0, len(places), 4):
+            add_particles(places[n : n + 4])
 
     def get_rows():
         for e in range(2):
@@ -369,7 +375,7 @@
     def get_particles(*places):
         for place in places:
             links.recv(("q",) + place, ints(*place), sibling)
-            add_particle(*place)
+        take_particles(*places)
 
 
     def first():
@@ -415,12 +421,12 @@
         step("own_sib", lambda: links.send(("S",), amp(0, 0, 0), sibling))
         step("own_sib_in", lambda: links.recv(("O",), amp(0, 0, 1), sibling))
         step("x0_send", x0_send, -1, "b", 1)
+        step("pair1", pair_send, 1)
         step("z_send", z_send, -1, "b", 1)
         step("x0_send", x0_send, 1, "f", 1)
         step("z_send", z_send, 1, "f", 1)
         step("x0_send", x0_send, -1, "b", 0)
         step("z_send", z_send, -1, "b", 0)
-        step("pair1", pair_send, 1)
         step("y_own1", y_send, 0, 1, 1)
         step("y01a", y_on, 0, 1, 0)
         step("x0", x0_first)
@@ -457,12 +463,12 @@
         step("h3", take_holes, (-1, 2), (1, 2))
         step("y14", y_on, 1, 4, 0)
         step("y14", y_on, 1, 4, 1)
-        step("p0", get_particles, (0, 0), (-1, 0), (1, 0), (0, -1), (0, 1), (0, 2), (2, 0))
+        step("p0", get_particles, (0, 0), (-1, 0), (1, 0), (0, -1))
         step("xf2", x_far, 2)
-        step("p1", get_particles, (-1, -1), (-1, 1), (1, -1), (1, 1))
+        step("p1", get_particles, (0, 1), (0, 2), (2, 0), (-1, -1))
         step("h3", take_holes, (2, 2))
-        step("p2", get_particles, (-1, 2), (1, 2), (2, -1), (2, 1))
-        step("p3", get_particles, (2, 2))
+        step("p2", get_particles, (-1, 1), (1, -1), (1, 1), (-1, 2))
+        step("p3", get_particles, (1, 2), (2, -1), (2, 1), (2, 2))
 
     def program_1():
         step("first", first)
@@ -470,15 +476,15 @@
         step("own_sib_in", lambda: links.recv(("S",), amp(0, 0, 0), sibling))
         step("first_in", first_in)
         step("second", second_out)
-        step("load", loads[1].wait)
-        step("h0", get_holes, (0, 0), (0, -1), (0, 1), (0, 2))
         step("second_in", second_in)
         step("p_own", p_own)
         step("ps0", p_sibs, (0, 0))
-        step("h1", get_holes, (-1, 0), (1, 0))
+        step("load", loads[1].wait)
         step("pa", pa_all)
         step("pb0", pb_all, 0)
         step("ps1", p_sibs, (0, 1), (0, -1), (1, 0), (-1, 0))
+        step("h0", get_holes, (0, 0), (0, -1), (0, 1))
+        step("h1", get_holes, (0, 2), (-1, 0), (1, 0))
         step("h1", get_holes, (2, 0))
         step("pa_far", pa_far)
         step("pbb0", pb_far, 0)
@@ -496,9 +502,8 @@
         step("ps5", p_sibs, (2, 2))
         step("h3", get_holes, (-1, 2), (1, 2))
         step("rows", get_rows)
-        step("p0", take_particles, (0, 0), (-1, 0), (1, 0), (0, -1), (0, 1), (0, 2), (2, 0))
-        step("p1", take_particles, (-1, -1), (-1, 1), (1, -1), (1, 1))
-        step("p2", take_particles, (-1, 2), (1, 2), (2, -1), (2, 1), (2, 2))
+        step("p0", take_particles, (0, 0), (-1, 0), (1, 0), (0, -1), (0, 1), (0, 2), (2, 0), (-1, -1))
+        step("p1", take_particles, (-1, 1), (1, -1), (1, 1), (-1, 2), (1, 2), (2, -1), (2, 1), (2, 2))
         step("h3", get_holes, (2, 2))
 
     def drain_0():
@@ -528,8 +533,7 @@
                 denom = virt_ref[:, cols] - occ_col[i * TILE : (i + 1) * TILE]
                 ladders = total[rows, cols]
                 res = keep * (direct[rows, cols].astype(jnp.float32) + ladders - denom * a)
-                residual_ref[rows, cols] = res
-                updated_ref[rows, cols] = (a + res / denom).astype(jnp.bfloat16)
+                step_ref[rows, cols] = res / denom
 
     step("finish", finish)
     pl.when(lead)(drain_0)
@@ -540,14 +544,11 @@
 
 def on_device(amplitudes, screen, hole_ints, particle_ints, direct_ints, occ_energy, virt_energy):
     vmem, hbm = pl.BlockSpec(memory_space=pltpu.VMEM), pl.BlockSpec(memory_space=pltpu.HBM)
-    return pl.pallas_call(
+    change = pl.pallas_call(
         kernel,
-        out_shape=(
-            jax.ShapeDtypeStruct((ROWS, COLS), jnp.float32),
-            jax.ShapeDtypeStruct((ROWS, COLS), jnp.bfloat16),
-        ),
+        out_shape=jax.ShapeDtypeStruct((ROWS, COLS), jnp.float32),
         in_specs=[hbm] * 7,
-        out_specs=(vmem, vmem),
+        out_specs=vmem,
         scratch_shapes=[
             pltpu.VMEM((ROWS, COLS), jnp.bfloat16),
             pltpu.VMEM((ROWS, COLS), jnp.bfloat16),
@@ -577,6 +578,8 @@
         occ_energy.reshape(1, ROWS),
         virt_energy.reshape(1, COLS),
     )
+    denom = virt_energy[None, :] - occ_energy[:, None]
+    return change * denom, (amplitudes.astype(jnp.float32) + change).astype(jnp.bfloat16)
 
 
 def solution(mesh):

time: 54.7 us -> 53.3 us (0.974)
  the two profiles are of different devices: /device:TPU:1 before, /device:TPU:91 now
where the time goes in v4:
time: 53.3 us; the launch traced here: 53.1 us
  Pallas kernels  50.7 us (95%)
  other arithmetic  1.76 us (3%)
  between operations  0.69 us (1%)
    pallas_call x1, Pallas kernels, on_device(): pl.pallas_call(kernel, out_shape=jax.ShapeDtypeStruct((ROWS, COLS), jnp.f...  50.7 us
    convert_element_type x1, other arithmetic, on_device(): (amplitudes.astype(jnp.float32) + change).astype(jnp.bfloat16)  1.76 us

profile of v4, /device:TPU:91, one launch (start us, length us, event | category | flops | bytes accessed | tf_op | source)
XLA Modules:
  0.0 53.1 jit_solution(7585914125176593944)
XLA Ops:
  0.6 0.0 copy-start.2
  0.6 0.0 copy-start.1
  0.7 0.0 copy-start
  0.7 50.7 %ladders.1 = f32[256,256]{1,0:T(8,128)} custom-call(s32[2,2]{1,0:T(2,128)} %screen_hbm.1, bf16[256,256]{1,0:T(8,128)(2,1)} %amps_hbm.1, bf16[256,8192]{1,0:T(8,128)(2,1)} %hole_hbm.1, bf16[256,128]{1,0:T(8,128)(2,1)} %part_hbm.1, bf16[256,256]{1,0:T(8,128)(2,1)} %direct_hbm.1, f32[1,256]{1,0:T(1,128)} %bitcast.2, f32[1,256]{1,0:T(1,128)} %bitcast.3), custom_call_target="tpu_custom_call" | custom-call | tf_op jit(solution)/shard_map/ladders/pallas_call | solution.py:547
  51.3 0.0 copy-done.2
  51.3 0.0 copy-done.1
  51.4 0.0 copy-done
  51.4 1.8 %add_convert_fusion = (bf16[256,256]{1,0:T(8,128)(2,1)}, f32[256,256]{1,0:T(8,128)}) fusion(f32[256,256]{1,0:T(8,128)} %ladders.1, bf16[256,256]{1,0:T(8,128)(2,1)S(1)} %copy-done, f32[256]{0:T(256)S(1)} %copy-done.1, f32[256]{0:T(256)S(1)} %copy-done.2), kind=kLoop, calls=%fused_computation | loop fusion | flops 327680 | bytes 788480 | tf_op jit(solution)/shard_map/convert_element_type | solution.py:582
Async XLA Ops:
  0.6 50.7 %copy-start.2 = (f32[256]{0:T(256)S(1)}, f32[256]{0:T(256)}, u32[]{:S(2)}) copy-start(f32[256]{0:T(256)} %param.13) | copy-start | bytes 3076
  0.6 50.7 %copy-start.1 = (f32[256]{0:T(256)S(1)}, f32[256]{0:T(256)}, u32[]{:S(2)}) copy-start(f32[256]{0:T(256)} %param.12) | copy-start | bytes 3076
  0.7 50.7 %copy-start = (bf16[256,256]{1,0:T(8,128)(2,1)S(1)}, bf16[256,256]{1,0:T(8,128)(2,1)}, u32[]{:S(2)}) copy-start(bf16[256,256]{1,0:T(8,128)(2,1)} %amps_hbm.1) | copy-start | bytes 393220

commit v5 on v4

--- a/solution.py
+++ b/solution.py
@@ -73,6 +73,7 @@
     occ_ref,
     virt_ref,
     screen,
+    part,
     send_sem,
     recv_sem,
     load_sem,
@@ -125,11 +126,13 @@
                 (occ_hbm, occ_ref),
                 (virt_hbm, virt_ref),
                 (screen_hbm, screen),
+                (part_hbm, part),
             )
         )
     ]
     loads[0].start()
     loads[5].start()
+    loads[6].start()
 
     barrier = pltpu.get_barrier_semaphore()
     for device in first_from:
@@ -143,6 +146,7 @@
     for load in loads[1:5]:
         load.start()
     loads[0].wait()
+    loads[6].wait()
     loads[5].wait()
     for i in range(2):
         for j in range(2):
@@ -379,29 +383,29 @@
 
 
     def first():
-        pl.when(lead)(lambda: links.send(("1", 0), part_hbm, first_to, moved.at[0]))
-        pl.when(other & first_moves)(lambda: links.send(("1", 1), part_hbm, first_to, moved.at[1]))
+        pl.when(lead)(lambda: links.send(("1", 0), part, first_to, moved.at[0]))
+        pl.when(other & first_moves)(lambda: links.send(("1", 1), part, first_to, moved.at[1]))
         pl.when(other & jnp.logical_not(first_moves))(
-            lambda: pltpu.make_async_copy(part_hbm, moved.at[1], load_sem.at[6]).start()
+            lambda: pltpu.make_async_copy(part, moved.at[1], load_sem.at[7]).start()
         )
 
     def first_in():
         links.recv(("1", 0), moved.at[0], first_from[0])
         pl.when(first_moves)(lambda: links.recv(("1", 1), moved.at[1], first_from[1]))
         pl.when(jnp.logical_not(first_moves))(
-            lambda: pltpu.make_async_copy(part_hbm, moved.at[1], load_sem.at[6]).wait()
+            lambda: pltpu.make_async_copy(part, moved.at[1], load_sem.at[7]).wait()
         )
 
     def second_out():
         pl.when(second_moves)(lambda: links.send(("2",), moved, second, ints(0, 0)))
         pl.when(jnp.logical_not(second_moves))(
-            lambda: pltpu.make_async_copy(moved, ints(0, 0), load_sem.at[7]).start()
+            lambda: pltpu.make_async_copy(moved, ints(0, 0), load_sem.at[8]).start()
         )
 
     def second_in():
         pl.when(second_moves)(lambda: links.recv(("2",), ints(0, 0), second))
         pl.when(jnp.logical_not(second_moves))(
-            lambda: pltpu.make_async_copy(moved, ints(0, 0), load_sem.at[7]).wait()
+            lambda: pltpu.make_async_copy(moved, ints(0, 0), load_sem.at[8]).wait()
         )
 
     def step(name, fn, *args, when=None):
@@ -561,9 +565,10 @@
             pltpu.VMEM((1, ROWS), jnp.float32),
             pltpu.VMEM((1, COLS), jnp.float32),
             pltpu.VMEM((2, 2), jnp.int32),
+            pltpu.VMEM((ROWS, TILE), jnp.bfloat16),
             pltpu.SemaphoreType.DMA((9,)),
             pltpu.SemaphoreType.DMA((N_COPIES,)),
-            pltpu.SemaphoreType.DMA((8,)),
+            pltpu.SemaphoreType.DMA((9,)),
         ],
         compiler_params=pltpu.CompilerParams(
             collective_id=0, has_side_effects=True, vmem_limit_bytes=62 * 2**20

time: 53.3 us -> 53 us (level)
  the two profiles are of different devices: /device:TPU:91 before, /device:TPU:1 now
where the time goes in v5:
time: 53 us; the launch traced here: 52.8 us
  Pallas kernels  50.4 us (95%)
  other arithmetic  1.76 us (3%)
  between operations  0.69 us (1%)
    pallas_call x1, Pallas kernels, on_device(): pl.pallas_call(kernel, out_shape=jax.ShapeDtypeStruct((ROWS, COLS), jnp.f...  50.4 us
    convert_element_type x1, other arithmetic, on_device(): (amplitudes.astype(jnp.float32) + change).astype(jnp.bfloat16)  1.76 us

profile of v5, /device:TPU:1, one launch (start us, length us, event | category | flops | bytes accessed | tf_op | source)
XLA Modules:
  0.0 52.8 jit_solution(9990576623053564196)
XLA Ops:
  0.6 0.0 copy-start.2
  0.6 0.0 copy-start.1
  0.7 0.0 copy-start
  0.7 50.4 %ladders.1 = f32[256,256]{1,0:T(8,128)} custom-call(s32[2,2]{1,0:T(2,128)} %screen_hbm.1, bf16[256,256]{1,0:T(8,128)(2,1)} %amps_hbm.1, bf16[256,8192]{1,0:T(8,128)(2,1)} %hole_hbm.1, bf16[256,128]{1,0:T(8,128)(2,1)} %part_hbm.1, bf16[256,256]{1,0:T(8,128)(2,1)} %direct_hbm.1, f32[1,256]{1,0:T(1,128)} %bitcast.2, f32[1,256]{1,0:T(1,128)} %bitcast.3), custom_call_target="tpu_custom_call" | custom-call | tf_op jit(solution)/shard_map/ladders/pallas_call | solution.py:551
  51.1 0.0 copy-done.2
  51.1 0.0 copy-done.1
  51.1 0.0 copy-done
  51.1 1.8 %add_convert_fusion = (bf16[256,256]{1,0:T(8,128)(2,1)}, f32[256,256]{1,0:T(8,128)}) fusion(f32[256,256]{1,0:T(8,128)} %ladders.1, bf16[256,256]{1,0:T(8,128)(2,1)S(1)} %copy-done, f32[256]{0:T(256)S(1)} %copy-done.1, f32[256]{0:T(256)S(1)} %copy-done.2), kind=kLoop, calls=%fused_computation | loop fusion | flops 327680 | bytes 788480 | tf_op jit(solution)/shard_map/convert_element_type | solution.py:587
Async XLA Ops:
  0.6 50.4 %copy-start.2 = (f32[256]{0:T(256)S(1)}, f32[256]{0:T(256)}, u32[]{:S(2)}) copy-start(f32[256]{0:T(256)} %param.13) | copy-start | bytes 3076
  0.6 50.4 %copy-start.1 = (f32[256]{0:T(256)S(1)}, f32[256]{0:T(256)}, u32[]{:S(2)}) copy-start(f32[256]{0:T(256)} %param.12) | copy-start | bytes 3076
  0.7 50.4 %copy-start = (bf16[256,256]{1,0:T(8,128)(2,1)S(1)}, bf16[256,256]{1,0:T(8,128)(2,1)}, u32[]{:S(2)}) copy-start(bf16[256,256]{1,0:T(8,128)(2,1)} %amps_hbm.1) | copy-start | bytes 393220
